TPU v7x, 32 devices: a whole 2x2x4 slice. The times are simulated.
32 devices in a mesh: slab: 16 (over z, y, x), kv: 2 (over core).
Axes of the slice: x: 2, y: 2, z: 4, core: 2. Of those that a mesh axis runs over, the one named last changes fastest.
Arguments:
- queries: bfloat16 [16384, 512], P('slab'), may hold values from -6 to 6
- grad_out: bfloat16 [16384, 512], P('slab'), may hold values from -6 to 6
- attn_out: bfloat16 [16384, 512], P('slab'), may hold values from -6 to 6
- row_lse: float32 [16384], P('slab'), may hold values from 5.5 to 7.5
- keys: bfloat16 [2, 2048, 512], P('kv', 'slab'), may hold values from -6 to 6
- values: bfloat16 [2, 2048, 512], P('kv', 'slab'), may hold values from -6 to 6
Outputs:
- grad_queries: bfloat16 [16384, 512], P('slab', 'kv')
- grad_keys: bfloat16 [2, 2048, 512], P('kv', 'slab')
- grad_values: bfloat16 [2, 2048, 512], P('kv', 'slab')
All inputs are finite; a program needn't handle non-finite values.
Results may differ from a plain program's by a relative error of at most 0.005.
Values may be sent and summed in bfloat16 or wider, within the bound.
A program may use at most 128 MiB of HBM per device.

v0:
```python
import jax
import jax.numpy as jnp
from jax import lax
from jax.sharding import PartitionSpec as P


def contract_last(left, right):
    return lax.dot_general(
        left, right, (((1,), (1,)), ((), ())), preferred_element_type=jnp.float32
    )


def contract_first(left, right):
    return lax.dot_general(
        left, right, (((0,), (0,)), ((), ())), preferred_element_type=jnp.float32
    )


def panel_work(query_rows, grad_rows, lse_rows, stats, panel_keys, panel_values, score_scale):
    scores = contract_last(query_rows, panel_keys) * score_scale
    probs = jnp.exp(scores - lse_rows[:, None])
    probs_low = probs.astype(jnp.bfloat16)
    dprobs = contract_last(grad_rows, panel_values)
    dscores = (probs * (dprobs - stats[:, None])).astype(jnp.bfloat16)
    grad_part = jnp.dot(dscores, panel_keys, preferred_element_type=jnp.float32) * score_scale
    return (grad_part, probs_low, dscores)


def on_device(queries, grad_out, attn_out, row_lse, keys, values):
    channels = queries.shape[1]
    score_scale = channels ** (-0.5)
    stats = jnp.sum(grad_out.astype(jnp.float32) * attn_out.astype(jnp.float32), axis=1)
    panel_keys, panel_values = (
        lax.all_gather(keys[0], "slab", axis=0, tiled=True),
        lax.all_gather(values[0], "slab", axis=0, tiled=True),
    )
    grad_part, probs_low, dscores = panel_work(
        queries, grad_out, row_lse, stats, panel_keys, panel_values, score_scale
    )
    grad_queries = lax.psum_scatter(grad_part, "kv", scatter_dimension=1, tiled=True).astype(
        jnp.bfloat16
    )
    key_grad = contract_first(dscores, queries) * score_scale
    value_grad = contract_first(probs_low, grad_out)
    combined = lax.psum_scatter(
        jnp.concatenate([key_grad, value_grad], axis=1), "slab", scatter_dimension=0, tiled=True
    )
    grad_keys = combined[:, :channels].astype(jnp.bfloat16)[None]
    grad_values = combined[:, channels:].astype(jnp.bfloat16)[None]
    return (grad_queries, grad_keys, grad_values)


def solution(mesh):
    placed = (
        P("slab", None),
        P("slab", None),
        P("slab", None),
        P("slab"),
        P("kv", "slab", None),
        P("kv", "slab", None),
    )
    return jax.shard_map(
        on_device,
        mesh=mesh,
        in_specs=placed,
        out_specs=(P("slab", "kv"), P("kv", "slab", None), P("kv", "slab", None)),
        check_vma=False,
    )
```

profile of v0, /device:TPU:0, one launch (start us, length us, event | category | flops | bytes accessed | tf_op | source)
XLA Modules:
  0.0 348.9 jit_solution(5371180529328590329)
XLA Ops:
  7.2 0.0 all-gather.5.cloned.1.call-start
  7.2 0.7 all-gather.5.cloned.1.call-update
  7.9 0.0 all-gather.7.cloned.1.call-start
  8.0 0.7 all-gather.7.cloned.1.call-update
  8.7 0.0 reduce-scatter.3.cloned.1.call-start
  8.7 1.9 multiply_reduce_fusion
  10.6 63.6 %all-gather.5.cloned.1.call-done = bf16[1,2048,512]{2,1,0:T(8,128)(2,1)} async-done(((bf16[1,128,512]{2,1,0:T(8,128)(2,1)}), bf16[1,2048,512]{2,1,0:T(8,128)(2,1)}) %all-gather.5.cloned.1.call-update) | async-done | bytes 2097168 | tf_op jit(solution)/shard_map/all_gather | solution.py:34
  74.2 7.2 %fusion.8 = f32[1024,2048]{1,0:T(8,128)} fusion(bf16[1024,512]{1,0:T(8,128)(2,1)S(1)} %copy-done, bf16[1,2048,512]{2,1,0:T(8,128)(2,1)} %all-gather.5.cloned.1.call-done), kind=kOutput, calls=%fused_computation.11 | convolution fusion | flops 2147483648 | bytes 11534336 | tf_op jit(solution)/shard_map/dot_general | solution.py:8
  81.4 55.0 %all-gather.7.cloned.1.call-done = bf16[1,2048,512]{2,1,0:T(8,128)(2,1)} async-done(((bf16[1,128,512]{2,1,0:T(8,128)(2,1)}), bf16[1,2048,512]{2,1,0:T(8,128)(2,1)}) %all-gather.7.cloned.1.call-update) | async-done | bytes 2097168 | tf_op jit(solution)/shard_map/all_gather | solution.py:35
  136.4 5.8 %multiply_convert_fusion = bf16[1024,2048]{1,0:T(8,128)(2,1)S(1)} fusion(f32[1024,2048]{1,0:T(8,128)} %fusion.8, f32[1024]{0:T(1024)S(1)} %multiply_reduce_fusion, f32[1024]{0:T(1024)S(1)} %copy-done.3, bf16[1024,512]{1,0:T(8,128)(2,1)S(1)} %copy-done.1, bf16[1,2048,512]{2,1,0:T(8,128)(2,1)} %all-gather.7.cloned.1.call-done), kind=kOutput, calls=%fused_computation.1 | convolution fusion | flops 2157969408 | bytes 15736832 | tf_op jit(solution)/shard_map/dot_general | solution.py:8
  142.2 2.0 copy-done.4
  144.2 3.7 %fusion.10 = f32[1024,512]{1,0:T(8,128)} fusion(bf16[1024,2048]{1,0:T(8,128)(2,1)S(1)} %multiply_convert_fusion, bf16[1,2048,512]{2,1,0:T(8,128)(2,1)S(1)} %copy-done.2), kind=kOutput, calls=%fused_computation.14 | convolution fusion | flops 2148007936 | bytes 8388608 | tf_op jit(solution)/shard_map/dot_general | solution.py:25
  147.8 0.0 reduce-scatter.3.cloned.1.call-update
  147.9 0.0 reduce-scatter.5.cloned.1.call-start
  147.9 4.6 %convolution_multiply_fusion = f32[2048,512]{0,1:T(8,128)S(1)} fusion(bf16[1024,2048]{1,0:T(8,128)(2,1)} %copy-done.4, bf16[1024,512]{1,0:T(8,128)(2,1)S(1)} %copy-done), kind=kOutput, calls=%fused_computation.7 | convolution fusion | flops 2148532224 | bytes 9437184 | tf_op jit(solution)/shard_map/dot_general | solution.py:14
  152.5 6.4 %fusion.1 = f32[2048,512]{0,1:T(8,128)S(1)} fusion(bf16[1024,512]{1,0:T(8,128)(2,1)S(1)} %copy-done.1, f32[1024,2048]{1,0:T(8,128)} %fusion.8, f32[1024]{0:T(1024)S(1)} %copy-done.3), kind=kOutput, calls=%fused_computation.4 | convolution fusion | flops 2153775104 | bytes 13635584 | tf_op jit(solution)/shard_map/dot_general | solution.py:14
  158.9 3.8 %pad_maximum_fusion = f32[2048,1024]{0,1:T(8,128)} fusion(f32[2048,512]{0,1:T(8,128)S(1)} %fusion.1, f32[2048,512]{0,1:T(8,128)S(1)} %convolution_multiply_fusion), kind=kLoop, calls=%fused_computation | loop fusion | flops 2097152 | bytes 16777216 | tf_op jit(solution)/shard_map/concatenate | solution.py:46
  162.7 0.0 reduce-scatter.5.cloned.1.call-update
  162.7 0.0 reduce-scatter.3.cloned.1.call-done
  162.7 2.1 convert_element_type.20
  164.8 175.0 %reduce-scatter.5.cloned.1.call-done = f32[128,1024]{0,1:T(8,128)} async-done(((f32[2048,1024]{0,1:T(8,128)}), f32[128,1024]{0,1:T(8,128)}) %reduce-scatter.5.cloned.1.call-update) | async-done | bytes 524304 | tf_op jit(solution)/shard_map/reduce_scatter | solution.py:45
  339.8 1.1 convert.4
  340.9 0.8 copy.9
  341.6 0.8 copy.10
  (10 shorter events, 0.0 us)
Async XLA Ops:
  7.2 67.1 %copy-start = (bf16[1024,512]{1,0:T(8,128)(2,1)S(1)}, bf16[1024,512]{1,0:T(8,128)(2,1)}, u32[]{:S(2)}) copy-start(bf16[1024,512]{1,0:T(8,128)(2,1)} %param.6) | copy-start | bytes 3145732
  7.2 67.0 %all-gather.5.cloned.1.call-start = ((), (), s32[]{:S(2)}) async-start(), calls=%async_computation.4 | async-start | bytes 2228224 | tf_op jit(solution)/shard_map/all_gather | solution.py:34
  7.9 128.5 %all-gather.7.cloned.1.call-start = ((), (), s32[]{:S(2)}) async-start(), calls=%async_computation.5 | async-start | bytes 2228224 | tf_op jit(solution)/shard_map/all_gather | solution.py:35
  8.7 154.1 %reduce-scatter.3.cloned.1.call-start = ((), (), s32[]{:S(2)}) async-start(), calls=%async_computation.2 | async-start | bytes 3145728 | tf_op jit(solution)/shard_map/reduce_scatter | solution.py:40
  10.6 125.8 %copy-start.1 = (bf16[1024,512]{1,0:T(8,128)(2,1)S(1)}, bf16[1024,512]{1,0:T(8,128)(2,1)}, u32[]{:S(2)}) copy-start(bf16[1024,512]{1,0:T(8,128)(2,1)} %param.7) | copy-start | bytes 3145732
  10.6 125.8 %copy-start.3 = (f32[1024]{0:T(1024)S(1)}, f32[1024]{0:T(1024)}, u32[]{:S(2)}) copy-start(f32[1024]{0:T(1024)} %param.9) | copy-start | bytes 12292
  136.4 7.8 %copy-start.2 = (bf16[1,2048,512]{2,1,0:T(8,128)(2,1)S(1)}, bf16[1,2048,512]{2,1,0:T(8,128)(2,1)}, u32[]{:S(2)}) copy-start(bf16[1,2048,512]{2,1,0:T(8,128)(2,1)} %all-gather.5.cloned.1.call-done) | copy-start | bytes 6291460
  142.2 2.0 copy-start.4
  147.9 191.9 %reduce-scatter.5.cloned.1.call-start = ((), (), s32[]{:S(2)}) async-start(), calls=%async_computation.3 | async-start | bytes 8912896 | tf_op jit(solution)/shard_map/reduce_scatter | solution.py:45
Sparse Core Ops, SparseCore 0:
  10.8 63.3 all-gather.4
  77.0 59.3 all-gather.6
  148.0 8.2 reduce-scatter.2
  162.8 176.8 reduce-scatter.4
where the time goes:
time: 351 us; the launch traced here: 349 us
  waiting for transfers between devices  295 us (84%)
  matrix products  27.6 us (8%)
  between operations  13.8 us (4%)
  other arithmetic  8.83 us (3%)
  local copies, waits for them, and re-layouts  3.55 us (1%)
    reduce_scatter x1, waiting for transfers between devices, on_device(): lax.psum_scatter(jnp.concatenate([key_grad, value_grad], axis=1), 'slab',...  175 us
    all_gather x1, waiting for transfers between devices, on_device(): lax.all_gather(keys[0], 'slab', axis=0, tiled=True)  63.6 us
    all_gather x1, waiting for transfers between devices, on_device(): lax.all_gather(values[0], 'slab', axis=0, tiled=True)  55 us
    dot_general x2, matrix products, contract_last(): lax.dot_general(left, right, (((1,), (1,)), ((), ())), preferred_element_...  13 us
    dot_general x2, matrix products, contract_first(): lax.dot_general(left, right, (((0,), (0,)), ((), ())), preferred_element_...  10.9 us
  transfers between devices with their start and end apart: 4, of which 3 were waited for; matrix products, arithmetic and copies ran while one was open for 7% of the time, Pallas kernels for 0%

commit v1 on v0

v1 whole, which is shorter than its diff:
```python
import functools
import math

import jax
import jax.numpy as jnp
from jax import lax
from jax.experimental import pallas as pl
from jax.experimental.pallas import tpu as pltpu
from jax.sharding import PartitionSpec as P

MESH = pl.DeviceIdType.MESH
F32 = jnp.float32
BF16 = jnp.bfloat16


def slab_layout(mesh):
    n_slab = mesh.shape["slab"]
    plain = ((n_slab, 1), (1, 1), (1, 1))
    try:
        coords = [tuple(d.coords) for d in mesh.devices[:, 0]]
    except (AttributeError, TypeError):
        return plain
    low = [min(c[p] for c in coords) for p in range(3)]
    coords = [tuple(c[p] - low[p] for p in range(3)) for c in coords]
    sizes = [max(c[p] for c in coords) + 1 for p in range(3)]
    if math.prod(sizes) != n_slab or len(set(coords)) != n_slab:
        return plain
    axes = []
    for p in range(3):
        unit = tuple(1 if q == p else 0 for q in range(3))
        axes.append((sizes[p], coords.index(unit) if sizes[p] > 1 else 1))
    for index, c in enumerate(coords):
        if any((index // axes[p][1]) % axes[p][0] != c[p] for p in range(3)):
            return plain
    (x, y, z) = axes
    return (z, y, x)


def kernel_body(
    layout, n_kv, scale,
    q_ref, do_ref, o_ref, lse_ref, k_ref, v_ref,
    dq_ref, dk_ref, dv_ref,
    kv, probs, dscores, acc, send_a, recv_a, send_b, recv_b, send_z, recv_z,
    dq_acc, dq_recv, rows,
    gz_s, gz_r, ga_s, ga_r, gb_s, gb_r, ra_s, ra_r, rb_s, rb_r, rz_s, rz_r, kv_s, kv_r,
):
    (nz, sz), (n_first, s_first), (n_second, s_second) = layout
    me = lax.axis_index("slab")
    core = lax.axis_index("kv")
    z = (me // sz) % nz
    first = (me // s_first) % n_first
    second = (me // s_second) % n_second
    na, nb = n_first, n_second
    if na == nb:
        odd = core % 2
        a = first + odd * (second - first)
        b = second + odd * (first - second)
        sa = s_first + odd * (s_second - s_first)
        sb = s_second + odd * (s_first - s_second)
    else:
        a, b, sa, sb = first, second, s_first, s_second
    kb = k_ref.shape[1]
    channels = k_ref.shape[2]
    tokens = q_ref.shape[0]
    col = nz * kb
    started = []

    def zp(d):
        return (z + d) % nz

    def ap(d):
        return (a + d) % na

    def bp(d):
        return (b + d) % nb

    def to_z(d):
        return (me + (zp(d) - z) * sz, core)

    def to_a(d):
        return (me + (ap(d) - a) * sa, core)

    def to_b(d):
        return (me + (bp(d) - b) * sb, core)

    def to_core(d):
        return (me, (core + d) % n_kv)

    def row(block):
        return pl.ds(pl.multiple_of(block * kb, kb), kb)

    def slot(rb, ra, rz):
        return row((bp(nb - rb) * na + ap(na - ra)) * nz + zp(nz - rz))

    def half(rb, rz):
        return row(bp(nb - rb) * nz + zp(nz - rz))

    def remote(src, dst, s, r, device):
        return pltpu.make_async_remote_copy(
            src_ref=src, dst_ref=dst, send_sem=s, recv_sem=r, device_id=device, device_id_type=MESH
        )

    def start(copy):
        copy.start()
        started.append(copy)

    peers = (
        [to_z(d) for d in range(1, nz)]
        + [to_a(d) for d in range(1, na)]
        + [to_b(d) for d in range(1, nb)]
        + [to_core(d) for d in range(1, n_kv)]
    )
    barrier = pltpu.get_barrier_semaphore()
    for peer in peers:
        pl.semaphore_signal(barrier, inc=1, device_id=peer, device_id_type=MESH)
    own = slot(0, 0, 0)
    kv[0, own, :] = k_ref[0]
    kv[1, own, :] = v_ref[0]
    pl.semaphore_wait(barrier, len(peers))

    def gather_z(d):
        s = kv.at[:, slot(0, 0, 0), :]
        return remote(s, s, gz_s.at[d - 1], gz_r.at[d - 1], to_z(d))

    def gather_a(d, rz):
        s = kv.at[:, slot(0, 0, rz), :]
        return remote(s, s, ga_s.at[d - 1, rz], ga_r.at[d - 1, rz], to_a(d))

    def gather_b(d, ra, rz):
        s = kv.at[:, slot(0, ra, rz), :]
        return remote(s, s, gb_s.at[d - 1, ra, rz], gb_r.at[d - 1, ra, rz], to_b(d))

    def arrived_z(d):
        s = kv.at[:, slot(0, 0, d), :]
        remote(s, s, gz_s.at[d - 1], gz_r.at[d - 1], to_z(d)).wait_recv()

    def arrived_a(d, rz):
        s = kv.at[:, slot(0, d, rz), :]
        remote(s, s, ga_s.at[d - 1, rz], ga_r.at[d - 1, rz], to_a(d)).wait_recv()

    def arrived_b(d, ra, rz):
        s = kv.at[:, slot(d, ra, rz), :]
        remote(s, s, gb_s.at[d - 1, ra, rz], gb_r.at[d - 1, ra, rz], to_b(d)).wait_recv()

    for d in range(1, nz):
        start(gather_z(d))
    for d in range(1, na):
        start(gather_a(d, 0))
    for d in range(1, nb):
        start(gather_b(d, 0, 0))

    qt = min(256, tokens)
    log2e = math.log2(math.e)

    @pl.loop(0, tokens // qt)
    def _(t):
        here = pl.ds(pl.multiple_of(t * qt, qt), qt)
        prod = do_ref[here, :].astype(F32) * o_ref[here, :].astype(F32)
        part = prod[:, :128]
        for lane in range(128, channels, 128):
            part = part + prod[:, lane : lane + 128]
        rows[1:2, here] = jnp.sum(part.T, axis=0, keepdims=True)
        rows[0:1, here] = lse_ref[:, here] * log2e

    for rz in range(1, nz):
        arrived_z(rz)
        for d in range(1, na):
            start(gather_a(d, rz))
        for d in range(1, nb):
            start(gather_b(d, 0, rz))

    kt = min(256, col)

    def column(rb, ra):
        top = pl.multiple_of((bp(nb - rb) * na + ap(na - ra)) * col, col)
        local = pl.multiple_of(bp(nb - rb) * col, col)

        @pl.loop(0, tokens // qt)
        def _(t):
            here = pl.ds(pl.multiple_of(t * qt, qt), qt)
            contract = (((1,), (1,)), ((), ()))
            span = pl.ds(top, col)
            s = lax.dot_general(kv[0, span, :], q_ref[here, :], contract, preferred_element_type=F32)
            p = jnp.exp2(s * (scale * log2e) - rows[0:1, here])
            dp = lax.dot_general(kv[1, span, :], do_ref[here, :], contract, preferred_element_type=F32)
            probs[:, here] = p.astype(BF16)
            dscores[span, here] = (p * (dp - rows[1:2, here])).astype(BF16)

        @pl.loop(0, col // kt)
        def _(t):
            off = t * kt
            span = pl.ds(pl.multiple_of(top + off, kt), kt)
            dk = jnp.dot(dscores[span, :], q_ref[...], preferred_element_type=F32)
            dv = jnp.dot(
                probs[pl.ds(pl.multiple_of(off, kt), kt), :], do_ref[...], preferred_element_type=F32
            )
            if ra == 0:
                there = pl.ds(pl.multiple_of(local + off, kt), kt)
                acc[0, there, :] = dk
                acc[1, there, :] = dv
            else:
                send_a[0, span, :] = dk.astype(BF16)
                send_a[1, span, :] = dv.astype(BF16)

    order_z = list(range(1, nz)) + [0]

    def reduce_a(ra, rb, rz):
        d = na - ra
        return remote(
            send_a.at[:, slot(rb, ra, rz), :], recv_a.at[d - 1, :, half(rb, rz), :],
            ra_s.at[d - 1, rb, rz], ra_r.at[d - 1, rb, rz], to_a(d),
        )

    def summed_a(d, rb, rz):
        here = half(rb, rz)
        dst = recv_a.at[d - 1, :, here, :]
        remote(dst, dst, ra_s.at[d - 1, rb, rz], ra_r.at[d - 1, rb, rz], to_a(d)).wait_recv()

    def reduce_b(rb, rz):
        d = nb - rb
        return remote(
            send_b.at[:, half(rb, rz), :], recv_b.at[d - 1, :, row(zp(nz - rz)), :],
            rb_s.at[d - 1, rz], rb_r.at[d - 1, rz], to_b(d),
        )

    def summed_b(d, rz):
        dst = recv_b.at[d - 1, :, row(zp(nz - rz)), :]
        remote(dst, dst, rb_s.at[d - 1, rz], rb_r.at[d - 1, rz], to_b(d)).wait_recv()

    def reduce_z(rz):
        d = nz - rz
        return remote(
            send_z.at[:, row(zp(d)), :], recv_z.at[d - 1], rz_s.at[d - 1], rz_r.at[d - 1], to_z(d)
        )

    column(0, 0)
    for rz in range(nz):
        for d in range(1, na):
            arrived_a(d, rz)
            for e in range(1, nb):
                start(gather_b(e, d, rz))
    for ra in range(1, na):
        column(0, ra)
        for rz in order_z:
            start(reduce_a(ra, 0, rz))
    for rb in range(1, nb):
        for rz in range(nz):
            arrived_b(rb, 0, rz)
        column(rb, 0)
    for rb in range(1, nb):
        for ra in range(1, na):
            for rz in range(nz):
                arrived_b(rb, ra, rz)
            column(rb, ra)
            for rz in order_z:
                start(reduce_a(ra, rb, rz))

    width = channels // n_kv

    @pl.loop(0, tokens // qt)
    def _(t):
        here = pl.ds(pl.multiple_of(t * qt, qt), qt)
        dq = lax.dot_general(
            dscores[:, here], kv[0], (((0,), (0,)), ((), ())), preferred_element_type=F32
        )
        for c in range(n_kv):
            dq_acc[c, here, :] = dq[:, c * width : (c + 1) * width]

    for d in range(1, n_kv):
        start(remote(
            dq_acc.at[(core + d) % n_kv], dq_recv.at[d - 1], kv_s.at[d - 1], kv_r.at[d - 1], to_core(d)
        ))

    def sum_a(rb, rz):
        here = half(rb, rz)
        total = acc[:, here, :]
        for d in range(1, na):
            summed_a(d, rb, rz)
            total = total + recv_a[d - 1, :, here, :].astype(F32)
        return total

    for rb in range(1, nb):
        for rz in order_z:
            send_b[:, half(rb, rz), :] = sum_a(rb, rz).astype(BF16)
            start(reduce_b(rb, rz))
    for rz in order_z:
        total = sum_a(0, rz)
        for d in range(1, nb):
            summed_b(d, rz)
            total = total + recv_b[d - 1, :, row(zp(nz - rz)), :].astype(F32)
        if rz != 0:
            send_z[:, row(zp(nz - rz)), :] = total.astype(BF16)
            start(reduce_z(rz))
        else:
            acc[:, half(0, 0), :] = total

    for d in range(1, n_kv):
        dst = dq_recv.at[d - 1]
        remote(dst, dst, kv_s.at[d - 1], kv_r.at[d - 1], to_core(d)).wait_recv()
    dq = dq_acc[core]
    for d in range(1, n_kv):
        dq = dq + dq_recv[d - 1]
    dq_ref[...] = (dq * scale).astype(BF16)

    total = acc[:, half(0, 0), :]
    for d in range(1, nz):
        dst = recv_z.at[d - 1]
        remote(dst, dst, rz_s.at[d - 1], rz_r.at[d - 1], to_z(d)).wait_recv()
        total = total + recv_z[d - 1].astype(F32)
    dk_ref[0] = (total[0] * scale).astype(BF16)
    dv_ref[0] = total[1].astype(BF16)
    for copy in started:
        copy.wait_send()


def solution(mesh):
    layout = slab_layout(mesh)
    n_kv = mesh.shape["kv"]
    (nz, _), (na, _), (nb, _) = layout

    def on_device(queries, grad_out, attn_out, row_lse, keys, values):
        tokens, channels = queries.shape
        kb = keys.shape[1]
        scale = channels ** (-0.5)
        col = nz * kb
        panel = na * nb * col
        width = channels // n_kv
        dma = pltpu.SemaphoreType.DMA

        def sems(*dims):
            dims = tuple(max(d, 1) for d in dims)
            return [dma(dims), dma(dims)]

        def buf(dtype, *dims):
            return pltpu.VMEM(tuple(max(d, 1) for d in dims), dtype)

        vmem = pl.BlockSpec(memory_space=pltpu.VMEM)
        return pl.pallas_call(
            functools.partial(kernel_body, layout, n_kv, scale),
            out_shape=(
                jax.ShapeDtypeStruct((tokens, width), BF16),
                jax.ShapeDtypeStruct(keys.shape, BF16),
                jax.ShapeDtypeStruct(values.shape, BF16),
            ),
            in_specs=[vmem] * 6,
            out_specs=(vmem,) * 3,
            scratch_shapes=[
                buf(BF16, 2, panel, channels),
                buf(BF16, col, tokens),
                buf(BF16, panel, tokens),
                buf(F32, 2, nb * col, channels),
                buf(BF16, 2, panel, channels),
                buf(BF16, na - 1, 2, nb * col, channels),
                buf(BF16, 2, nb * col, channels),
                buf(BF16, nb - 1, 2, col, channels),
                buf(BF16, 2, col, channels),
                buf(BF16, nz - 1, 2, kb, channels),
                buf(F32, n_kv, tokens, width),
                buf(F32, n_kv - 1, tokens, width),
                buf(F32, 8, tokens),
                *sems(nz - 1),
                *sems(na - 1, nz),
                *sems(nb - 1, na, nz),
                *sems(na - 1, nb, nz),
                *sems(nb - 1, nz),
                *sems(nz - 1),
                *sems(n_kv - 1),
            ],
            compiler_params=pltpu.CompilerParams(
                collective_id=0, has_side_effects=True, vmem_limit_bytes=56 * 1024 * 1024
            ),
            name="attention_backward",
        )(queries, grad_out, attn_out, row_lse.reshape(1, tokens), keys, values)

    placed = (
        P("slab", None),
        P("slab", None),
        P("slab", None),
        P("slab"),
        P("kv", "slab", None),
        P("kv", "slab", None),
    )
    return jax.shard_map(
        on_device,
        mesh=mesh,
        in_specs=placed,
        out_specs=(P("slab", "kv"), P("kv", "slab", None), P("kv", "slab", None)),
        check_vma=False,
    )
```

time: 351 us -> 111 us (0.32)
  waiting for transfers between devices: 295 us -> 0 us
  Pallas kernels: 0 us -> 106 us
  matrix products: 27.6 us -> 0 us
  between operations: 13.8 us -> 0.65 us
  other arithmetic: 8.83 us -> 0 us
    reduce_scatter x2 -> x0, waiting for transfers between devices: 175 us -> none  [the longest x1 175 us: on_device(): lax.psum_scatter(jnp.concatenate([key_grad, value_grad], axis=1), 'slab',...]
    all_gather x2 -> x0, waiting for transfers between devices: 119 us -> none  [the longest x1 63.6 us: on_device(): lax.all_gather(keys[0], 'slab', axis=0, tiled=True)]
    pallas_call x0 -> x1, Pallas kernels: none -> 106 us  [on_device(): pl.pallas_call(functools.partial(kernel_body, layout, n_kv, scale), out_s...]
    dot_general x5 -> x0, matrix products: 27.6 us -> none  [the longest x2 13 us: contract_last(): lax.dot_general(left, right, (((1,), (1,)), ((), ())), preferred_element_...]
    concatenate x1 -> x0, other arithmetic: 3.81 us -> none  [on_device(): jnp.concatenate([key_grad, value_grad], axis=1)]
  transfers between devices with their start and end apart: 4 -> 0, of which waited for: 3 -> 0; matrix products, arithmetic and copies ran while one was open for 7% -> 0% of each run, Pallas kernels for 0% -> 0%
where the time goes in v1:
time: 111 us; the launch traced here: 110 us
  Pallas kernels  106 us (95%)
  local copies, waits for them, and re-layouts  3.51 us (3%)
    pallas_call x1, Pallas kernels, on_device(): pl.pallas_call(functools.partial(kernel_body, layout, n_kv, scale), out_s...  106 us
    unnamed x7, local copies, waits for them, and re-layouts  3.51 us

profile of v1, /device:TPU:0, one launch (start us, length us, event | category | flops | bytes accessed | tf_op | source)
XLA Modules:
  0.0 110.4 jit_solution(12466766866515711232)
XLA Ops:
  0.6 106.2 %attention_backward.1 = (bf16[1024,256]{1,0:T(8,128)(2,1)}, bf16[1,128,512]{2,1,0:T(8,128)(2,1)}, bf16[1,128,512]{2,1,0:T(8,128)(2,1)}) custom-call(bf16[1024,512]{1,0:T(8,128)(2,1)} %q_ref.1, bf16[1024,512]{1,0:T(8,128)(2,1)} %do_ref.1, bf16[1024,512]{1,0:T(8,128)(2,1)} %o_ref.1, f32[1,1024]{1,0:T(1,128)} %bitcast.1, bf16[1,128,512]{2,1,0:T(8,128)(2,1)} %k_ref.1, ...), custom_call_target="tpu_custom_call" | custom-call | tf_op jit(solution)/shard_map/attention_backward/pallas_call | solution.py:338
  106.8 0.0 copy-start.1
  106.9 1.9 %copy.12 = bf16[1024,256]{1,0:T(8,128)(2,1)} copy(bf16[1024,256]{1,0:T(8,128)(2,1)} %get-tuple-element.6) | data formatting | bytes 1048576
  108.8 0.0 copy-done.1
  108.8 0.0 copy-start
  108.8 0.7 copy.13
  109.4 0.3 copy-done
  109.7 0.7 copy.14
Async XLA Ops:
  106.8 1.9 %copy-start.1 = (bf16[1,128,512]{2,1,0:T(8,128)(2,1)S(1)}, bf16[1,128,512]{2,1,0:T(8,128)(2,1)}, u32[]{:S(2)}) copy-start(bf16[1,128,512]{2,1,0:T(8,128)(2,1)} %get-tuple-element.7) | copy-start | bytes 393220
  108.8 1.0 copy-start

commit v2 on v1

--- a/solution.py
+++ b/solution.py
@@ -118,36 +118,78 @@
     kv[1, own, :] = v_ref[0]
     pl.semaphore_wait(barrier, len(peers))
 
-    def gather_z(d):
-        s = kv.at[:, slot(0, 0, 0), :]
-        return remote(s, s, gz_s.at[d - 1], gz_r.at[d - 1], to_z(d))
-
-    def gather_a(d, rz):
-        s = kv.at[:, slot(0, 0, rz), :]
-        return remote(s, s, ga_s.at[d - 1, rz], ga_r.at[d - 1, rz], to_a(d))
-
-    def gather_b(d, ra, rz):
-        s = kv.at[:, slot(0, ra, rz), :]
-        return remote(s, s, gb_s.at[d - 1, ra, rz], gb_r.at[d - 1, ra, rz], to_b(d))
-
-    def arrived_z(d):
-        s = kv.at[:, slot(0, 0, d), :]
-        remote(s, s, gz_s.at[d - 1], gz_r.at[d - 1], to_z(d)).wait_recv()
-
-    def arrived_a(d, rz):
-        s = kv.at[:, slot(0, d, rz), :]
-        remote(s, s, ga_s.at[d - 1, rz], ga_r.at[d - 1, rz], to_a(d)).wait_recv()
-
-    def arrived_b(d, ra, rz):
-        s = kv.at[:, slot(d, ra, rz), :]
-        remote(s, s, gb_s.at[d - 1, ra, rz], gb_r.at[d - 1, ra, rz], to_b(d)).wait_recv()
-
-    for d in range(1, nz):
-        start(gather_z(d))
-    for d in range(1, na):
-        start(gather_a(d, 0))
-    for d in range(1, nb):
-        start(gather_b(d, 0, 0))
+    def block(rb, ra, zb):
+        return row((bp(nb - rb) * na + ap(na - ra)) * nz + zb)
+
+    def line_z(way, t, zb):
+        s = kv.at[:, block(0, 0, zb), :]
+        return remote(s, s, gz_s.at[way, t], gz_r.at[way, t], (me + (1 - 2 * way) * sz, core))
+
+    def gather_a(d, zb):
+        s = kv.at[:, block(0, 0, zb), :]
+        return remote(s, s, ga_s.at[d - 1, zb], ga_r.at[d - 1, zb], to_a(d))
+
+    def gather_b(d, ra, zb):
+        s = kv.at[:, block(0, ra, zb), :]
+        return remote(s, s, gb_s.at[d - 1, ra, zb], gb_r.at[d - 1, ra, zb], to_b(d))
+
+    def arrived_a(d, zb):
+        s = kv.at[:, block(0, d, zb), :]
+        remote(s, s, ga_s.at[d - 1, zb], ga_r.at[d - 1, zb], to_a(d)).wait_recv()
+
+    def arrived_b(d, ra, zb):
+        s = kv.at[:, block(d, ra, zb), :]
+        remote(s, s, gb_s.at[d - 1, ra, zb], gb_r.at[d - 1, ra, zb], to_b(d)).wait_recv()
+
+    def from_z(way, t):
+        zb = z - 1 - t if way == 0 else z + 1 + t
+        return zb, (zb >= 0 if way == 0 else zb < nz)
+
+    def has_next(way):
+        return z + 1 < nz if way == 0 else z >= 1
+
+    def spread(zb):
+        for d in range(1, na):
+            gather_a(d, zb).start()
+        for d in range(1, nb):
+            gather_b(d, 0, zb).start()
+
+    def pass_b(zb):
+        for d in range(1, na):
+            arrived_a(d, zb)
+            for e in range(1, nb):
+                gather_b(e, d, zb).start()
+
+    def step_z(t):
+        for way in range(2):
+            zb, there = from_z(way, t)
+
+            @pl.when(there)
+            def _():
+                s = kv.at[:, block(0, 0, zb), :]
+                remote(
+                    s, s, gz_s.at[way, t], gz_r.at[way, t], (me + (2 * way - 1) * sz, core)
+                ).wait_recv()
+                if t + 1 < nz - 1:
+                    @pl.when(has_next(way))
+                    def _():
+                        line_z(way, t + 1, zb).start()
+                spread(zb)
+
+    def step_a(t):
+        for way in range(2):
+            zb, there = from_z(way, t)
+
+            @pl.when(there)
+            def _():
+                pass_b(zb)
+
+    if nz > 1:
+        for way in range(2):
+            @pl.when(has_next(way))
+            def _():
+                line_z(way, 0, z).start()
+    spread(z)
 
     qt = min(256, tokens)
     log2e = math.log2(math.e)
@@ -162,12 +204,14 @@
         rows[1:2, here] = jnp.sum(part.T, axis=0, keepdims=True)
         rows[0:1, here] = lse_ref[:, here] * log2e
 
-    for rz in range(1, nz):
-        arrived_z(rz)
-        for d in range(1, na):
-            start(gather_a(d, rz))
-        for d in range(1, nb):
-            start(gather_b(d, 0, rz))
+    for t in range(nz - 1):
+        step_z(t)
+        if t == 0:
+            pass_b(z)
+        else:
+            step_a(t - 1)
+    if nz == 1:
+        pass_b(z)
 
     kt = min(256, col)
 
@@ -234,25 +278,23 @@
         )
 
     column(0, 0)
-    for rz in range(nz):
-        for d in range(1, na):
-            arrived_a(d, rz)
-            for e in range(1, nb):
-                start(gather_b(e, d, rz))
+    if nz > 1:
+        step_a(nz - 2)
     for ra in range(1, na):
         column(0, ra)
         for rz in order_z:
             start(reduce_a(ra, 0, rz))
     for rb in range(1, nb):
-        for rz in range(nz):
-            arrived_b(rb, 0, rz)
+        for zb in range(nz):
+            arrived_b(rb, 0, zb)
         column(rb, 0)
+    ahead = 2
     for rb in range(1, nb):
         for ra in range(1, na):
-            for rz in range(nz):
-                arrived_b(rb, ra, rz)
+            for zb in range(nz):
+                arrived_b(rb, ra, zb)
             column(rb, ra)
-            for rz in order_z:
+            for rz in order_z[:ahead]:
                 start(reduce_a(ra, rb, rz))
 
     width = channels // n_kv
@@ -279,11 +321,7 @@
             total = total + recv_a[d - 1, :, here, :].astype(F32)
         return total
 
-    for rb in range(1, nb):
-        for rz in order_z:
-            send_b[:, half(rb, rz), :] = sum_a(rb, rz).astype(BF16)
-            start(reduce_b(rb, rz))
-    for rz in order_z:
+    def finish(rz):
         total = sum_a(0, rz)
         for d in range(1, nb):
             summed_b(d, rz)
@@ -294,6 +332,18 @@
         else:
             acc[:, half(0, 0), :] = total
 
+    for k, rz in enumerate(order_z):
+        for rb in range(1, nb):
+            total = sum_a(rb, rz)
+            if k + ahead < nz:
+                for ra in range(1, na):
+                    start(reduce_a(ra, rb, order_z[k + ahead]))
+            send_b[:, half(rb, rz), :] = total.astype(BF16)
+            start(reduce_b(rb, rz))
+        if k > 0:
+            finish(order_z[k - 1])
+    finish(order_z[-1])
+
     for d in range(1, n_kv):
         dst = dq_recv.at[d - 1]
         remote(dst, dst, kv_s.at[d - 1], kv_r.at[d - 1], to_core(d)).wait_recv()
@@ -311,6 +361,20 @@
     dv_ref[0] = total[1].astype(BF16)
     for copy in started:
         copy.wait_send()
+    for zb in range(nz):
+        for d in range(1, na):
+            gather_a(d, zb).wait_send()
+        for d in range(1, nb):
+            for ra in range(na):
+                gather_b(d, ra, zb).wait_send()
+    for t in range(nz - 1):
+        for way in range(2):
+            zb = z - t if way == 0 else z + t
+            held = jnp.logical_and(has_next(way), zb >= 0 if way == 0 else zb < nz)
+
+            @pl.when(held)
+            def _():
+                line_z(way, t, zb).wait_send()
 
 
 def solution(mesh):
@@ -358,7 +422,7 @@
                 buf(F32, n_kv, tokens, width),
                 buf(F32, n_kv - 1, tokens, width),
                 buf(F32, 8, tokens),
-                *sems(nz - 1),
+                *sems(2, nz - 1),
                 *sems(na - 1, nz),
                 *sems(nb - 1, na, nz),
                 *sems(na - 1, nb, nz),

time: 111 us -> 96.1 us (0.87)
  Pallas kernels: 106 us -> 91.8 us
    pallas_call x1, Pallas kernels: 106 us -> 91.8 us  [on_device(): pl.pallas_call(functools.partial(kernel_body, layout, n_kv, scale), out_s...]
where the time goes in v2:
time: 96.1 us; the launch traced here: 96 us
  Pallas kernels  91.8 us (96%)
  local copies, waits for them, and re-layouts  3.51 us (4%)
    pallas_call x1, Pallas kernels, on_device(): pl.pallas_call(functools.partial(kernel_body, layout, n_kv, scale), out_s...  91.8 us
    unnamed x7, local copies, waits for them, and re-layouts  3.51 us

profile of v2, /device:TPU:0, one launch (start us, length us, event | category | flops | bytes accessed | tf_op | source)
XLA Modules:
  0.0 96.0 jit_solution(10656026724697989591)
XLA Ops:
  0.6 91.8 %attention_backward.1 = (bf16[1024,256]{1,0:T(8,128)(2,1)}, bf16[1,128,512]{2,1,0:T(8,128)(2,1)}, bf16[1,128,512]{2,1,0:T(8,128)(2,1)}) custom-call(bf16[1024,512]{1,0:T(8,128)(2,1)} %q_ref.1, bf16[1024,512]{1,0:T(8,128)(2,1)} %do_ref.1, bf16[1024,512]{1,0:T(8,128)(2,1)} %o_ref.1, f32[1,1024]{1,0:T(1,128)} %bitcast.1, bf16[1,128,512]{2,1,0:T(8,128)(2,1)} %k_ref.1, ...), custom_call_target="tpu_custom_call" | custom-call | tf_op jit(solution)/shard_map/attention_backward/pallas_call | solution.py:402
  92.4 0.0 copy-start.1
  92.4 1.9 %copy.12 = bf16[1024,256]{1,0:T(8,128)(2,1)} copy(bf16[1024,256]{1,0:T(8,128)(2,1)} %get-tuple-element.6) | data formatting | bytes 1048576
  94.3 0.0 copy-done.1
  94.4 0.0 copy-start
  94.4 0.7 copy.13
  95.0 0.3 copy-done
  95.3 0.7 copy.14
Async XLA Ops:
  92.4 1.9 %copy-start.1 = (bf16[1,128,512]{2,1,0:T(8,128)(2,1)S(1)}, bf16[1,128,512]{2,1,0:T(8,128)(2,1)}, u32[]{:S(2)}) copy-start(bf16[1,128,512]{2,1,0:T(8,128)(2,1)} %get-tuple-element.7) | copy-start | bytes 393220
  94.4 1.0 copy-start
